TPU v7x, 256 devices: a whole 4x4x8 slice. The times are simulated.
256 devices in a mesh: outer: 8 (over y, x_lo), inner: 8 (over z), fsdp: 4 (over x_hi, core).
Axes of the slice: x: 4 (x_hi: 2, x_lo: 2; x = x_hi * 2 + x_lo), y: 4, z: 8, core: 2. Of those that a mesh axis runs over, the one named last changes fastest.
Arguments:
- hidden_in: bfloat16 [4, 8192, 2304], P('fsdp', ('outer', 'inner')), may hold values from -16 to 16
- queries: bfloat16 [4, 8192, 2048], P('fsdp', ('outer', 'inner')), may hold values from -14 to 14, as said below
- keys: bfloat16 [4, 8192, 1024], P('fsdp', ('outer', 'inner')), may hold values from -5 to 5, as said below
- values: bfloat16 [4, 8192, 1024], P('fsdp', ('outer', 'inner')), may hold values from -6 to 6
- fwd_out: bfloat16 [4, 8192, 2048], P('fsdp', ('outer', 'inner')), may hold values from -6 to 6
- out_grad: bfloat16 [4, 8192, 2048], P('fsdp', ('outer', 'inner')), may hold values from -6 to 6
- lse: float32 [4, 16, 8192], P('fsdp', None, ('outer', 'inner')), may hold values from 20 to 60, as said below
- block_order: int32 [64], replicated, may hold values from 0 to 63, each once
- doc_lengths: int32 [4, 4], P('fsdp'), may hold values from 1 to 4096, 8192 in all within a row
Outputs:
- qkv_grads: bfloat16 [4, 8192, 4096], P('fsdp', ('outer', 'inner'))
- weight_grads: bfloat16 [8, 2304, 4096], P('outer', ('inner', 'fsdp'))
Inputs may be any that keep to these rules, and one draw needn't show every extreme that they name: `block_order`: each context slot holds a different block. `doc_lengths`: the documents of one sequence cover it in order; one of them spans 4096 positions. `queries`: saved from the forward pass. `keys`: saved from the forward pass. `lse`: saved from the forward pass.
All inputs are finite; a program needn't handle non-finite values.
Results may differ from a plain program's by a relative error of at most 0.02.
Values may be sent and summed in bfloat16 or wider, within the bound.
A program may use at most 128 MiB of HBM per device.

v0:
```python
import jax
import jax.numpy as jnp
from jax import lax
from jax.sharding import PartitionSpec as P

HQ = 16
HK = 8
HD = 128


softcap = 50.0
query_scale = 144.0 ** (-0.5)


def from_behind(x, axis, by):
    devices = lax.axis_size(axis)
    return lax.ppermute(x, axis, [(i, (i + by) % devices) for i in range(devices)])


def rope_back(grad, pos, heads, head_size):
    tok = grad.shape[0]
    half = head_size // 2
    g = grad.reshape(tok, heads, head_size)
    inv = 10000.0 ** (-2.0 * jnp.arange(half).astype(jnp.float32) / head_size)
    angle = pos.astype(jnp.float32)[:, None] * inv[None, :]
    cosv = jnp.cos(angle)[:, None, :]
    sinv = jnp.sin(angle)[:, None, :]
    g1 = g[:, :, :half]
    g2 = g[:, :, half:]
    return jnp.concatenate([g1 * cosv + g2 * sinv, g2 * cosv - g1 * sinv], axis=-1).reshape(
        tok, heads * head_size
    )


def local(hidden_in, queries, keys, values, fwd_out, out_grad, lse, block_order, doc_lengths):
    n_outer = lax.axis_size("outer")
    n_inner = lax.axis_size("inner")
    outer_at = lax.axis_index("outer")
    inner_at = lax.axis_index("inner")
    tok = queries.shape[1]
    kv_heads = HK
    groups = HQ // HK
    head_size = HD
    lengths = doc_lengths[0]
    starts = jnp.cumsum(lengths) - lengths
    steps_in = jnp.arange(tok, dtype=jnp.int32)

    def slot_positions(outer_pos, inner_pos):
        slot = outer_pos % n_outer * n_inner + inner_pos % n_inner
        pos = block_order[slot] * tok + steps_in
        doc = jnp.sum((pos[:, None] >= starts[None, :]).astype(jnp.int32), axis=1)
        return (pos, doc)

    qpos, qdoc = slot_positions(outer_at, inner_at)
    qb = queries[0].reshape(tok, kv_heads, groups, head_size)
    dob = out_grad[0].reshape(tok, kv_heads, groups, head_size)
    lse_b = lse[0].reshape(kv_heads, groups, tok)
    delta = out_grad[0].astype(jnp.float32) * fwd_out[0].astype(jnp.float32)
    delta = delta.reshape(tok, kv_heads, groups, head_size).sum(-1).transpose(1, 2, 0)

    def attend(kv_pair, kpos, kdoc):
        kb = kv_pair[0].reshape(tok, kv_heads, head_size)
        vb = kv_pair[1].reshape(tok, kv_heads, head_size)
        raw = jnp.einsum("qhgd,khd->hgqk", qb, kb, preferred_element_type=jnp.float32) * query_scale
        capped = jnp.tanh(raw / softcap)
        live = (kpos[None, :] <= qpos[:, None]) & (kdoc[None, :] == qdoc[:, None])
        prob = jnp.where(
            live[None, None], jnp.exp(softcap * capped - lse_b[:, :, :, None]), jnp.float32(0.0)
        )
        prob_b = prob.astype(jnp.bfloat16)
        dprob = jnp.einsum("qhgd,khd->hgqk", dob, vb, preferred_element_type=jnp.float32)
        dscore = (
            prob * (dprob - delta[:, :, :, None]) * (1.0 - capped * capped) * query_scale
        ).astype(jnp.bfloat16)
        dq = jnp.einsum("hgqk,khd->qhgd", dscore, kb, preferred_element_type=jnp.float32).reshape(
            tok, HQ * head_size
        )
        dk = jnp.einsum("hgqk,qhgd->khd", dscore, qb, preferred_element_type=jnp.float32).reshape(
            tok, kv_heads * head_size
        )
        dv = jnp.einsum("hgqk,qhgd->khd", prob_b, dob, preferred_element_type=jnp.float32).reshape(
            tok, kv_heads * head_size
        )
        return (dq, jnp.stack([dk, dv]))

    def rotate(kv_pair):
        return from_behind(kv_pair, "inner", 1)

    kv_home = jnp.stack([keys[0], values[0]])
    kv_one = rotate(kv_home)
    kv_two = rotate(kv_one)
    kv_prior = from_behind(kv_home, "outer", 1)
    dq_home, part_home = attend(kv_home, qpos, qdoc)
    pos_one, doc_one = slot_positions(outer_at, inner_at - 1)
    dq_one, part_one = attend(kv_one, pos_one, doc_one)
    pos_two, doc_two = slot_positions(outer_at, inner_at - 2)
    dq_two, part_two = attend(kv_two, pos_two, doc_two)
    pos_prior, doc_prior = slot_positions(outer_at - 1, inner_at)
    dq_prior, part_prior = attend(kv_prior, pos_prior, doc_prior)
    dq_total = dq_home + dq_one + dq_two + dq_prior
    dq_grads = rope_back(dq_total, qpos, HQ, head_size).astype(jnp.bfloat16)
    x_rows = hidden_in[0]

    def backward(partial_value):
        return from_behind(partial_value.astype(jnp.bfloat16), "inner", -1).astype(
            partial_value.dtype
        )

    carried = backward(part_two) + part_one
    carried = backward(carried) + part_home
    carried = carried + from_behind(part_prior.astype(jnp.bfloat16), "outer", -1).astype(
        part_prior.dtype
    )
    dk_grads = rope_back(carried[0], qpos, kv_heads, head_size).astype(jnp.bfloat16)
    dv_grads = carried[1].astype(jnp.bfloat16)
    kv_grads = jnp.concatenate([dk_grads, dv_grads], axis=1)
    all_grads = jnp.concatenate([dq_grads, kv_grads], axis=1)
    weight_rows = lax.psum_scatter(
        lax.dot_general(
            x_rows, all_grads, (((0,), (0,)), ((), ())), preferred_element_type=jnp.float32
        ).astype(jnp.bfloat16),
        ("inner", "fsdp"),
        scatter_dimension=0,
        tiled=True,
    )
    return (all_grads[None], weight_rows[None])


def solution(mesh):
    in_specs = (
        P("fsdp", ("outer", "inner"), None),
        P("fsdp", ("outer", "inner"), None),
        P("fsdp", ("outer", "inner"), None),
        P("fsdp", ("outer", "inner"), None),
        P("fsdp", ("outer", "inner"), None),
        P("fsdp", ("outer", "inner"), None),
        P("fsdp", None, ("outer", "inner")),
        P(),
        P("fsdp", None),
    )
    out_specs = (P("fsdp", ("outer", "inner"), None), P("outer", ("inner", "fsdp"), None))
    return jax.shard_map(local, mesh=mesh, in_specs=in_specs, out_specs=out_specs, check_vma=False)
```

profile of v0, /device:TPU:1, one launch (start us, length us, event | category | flops | bytes accessed | tf_op | source)
XLA Modules:
  0.0 381.0 jit_solution(1147238915105684505)
XLA Ops:
  7.3 1.2 copy.167
  10.5 2.0 collective-permute-start.2
  12.5 1.6 collective-permute-start
  21.9 1.5 compare_and_fusion.1
  24.1 1.8 fusion.47
  25.9 2.0 copy.202
  28.0 3.1 reshape.344
  31.0 3.2 multiply_reduce_fusion
  34.2 1.8 copy.164
  36.0 1.5 fusion.24
  38.9 1.3 convolution_bitcast_fusion
  40.1 1.8 fusion.83
  43.4 2.0 copy.196
  45.5 1.8 fusion.84
  50.5 2.5 fusion.25
  53.6 1.9 collective-permute-start.1
  58.0 1.8 pad_maximum_fusion.4
  59.8 2.5 collective-permute-start.5
  62.3 7.2 %collective-permute-done.1 = bf16[2,128,1024]{1,2,0:T(8,128)(2,1)} collective-permute-done((bf16[2,128,1024]{1,2,0:T(8,128)(2,1)}, bf16[2,128,1024]{1,2,0:T(8,128)(2,1)}, u32[]{:S(2)}, u32[]{:S(2)}) %collective-permute-start.1) | collective-permute-done | bytes 524320 | tf_op jit(solution)/shard_map/ppermute | solution.py:17
  69.5 1.8 fusion.82
  72.7 1.8 copy.190
  74.5 1.5 fusion.26
  79.3 1.2 collective-permute-start.3
  81.1 10.1 %collective-permute-done.3 = bf16[2,128,1024]{2,1,0:T(8,128)(2,1)S(1)} collective-permute-done((bf16[2,128,1024]{2,1,0:T(8,128)(2,1)S(1)}, bf16[2,128,1024]{2,1,0:T(8,128)(2,1)S(1)}, u32[]{:S(2)}, u32[]{:S(2)}) %collective-permute-start.3) | collective-permute-done | bytes 524320 | tf_op jit(solution)/shard_map/ppermute | solution.py:17
  92.2 2.0 collective-permute-start.4
  94.9 8.4 %collective-permute-done.4 = bf16[2,128,1024]{2,1,0:T(8,128)(2,1)S(1)} collective-permute-done((bf16[2,128,1024]{2,1,0:T(8,128)(2,1)}, bf16[2,128,1024]{2,1,0:T(8,128)(2,1)S(1)}, u32[]{:S(2)}, u32[]{:S(2)}) %collective-permute-start.4) | collective-permute-done | bytes 524320 | tf_op jit(solution)/shard_map/ppermute | solution.py:17
  103.3 1.3 fusion.33
  106.0 9.2 %fusion = bf16[2304,4096]{0,1:T(8,128)(2,1)} fusion(bf16[1,128,2304]{2,1,0:T(8,128)(2,1)S(1)} %copy-done, bf16[128,1024]{1,0:T(8,128)(2,1)S(1)} %fusion.70, bf16[128,1024]{1,0:T(8,128)(2,1)S(1)} %bitcast.296, bf16[128,2048]{1,0:T(8,128)(2,1)S(1)} %copy.262), kind=kOutput, calls=%fused_computation.1 | convolution fusion | flops 2428502016 | bytes 20512768 | tf_op jit(solution)/shard_map/dot_general | solution.py:119
  115.2 23.4 %copy.263 = bf16[2304,4096]{1,0:T(8,128)(2,1)} copy(bf16[2304,4096]{0,1:T(8,128)(2,1)} %fusion) | data formatting | bytes 37748736
  139.7 231.7 %reduce-scatter.4.cloned.1.call-done = bf16[72,4096]{1,0:T(8,128)(2,1)} async-done(((bf16[2304,4096]{1,0:T(8,128)(2,1)}), bf16[72,4096]{1,0:T(8,128)(2,1)}) %reduce-scatter.4.cloned.1.call-update) | async-done | bytes 589840
  371.4 1.5 copy.264
  372.9 1.2 copy.211
  (126 shorter events, 26.1 us)
Async XLA Ops:
  7.2 98.8 %copy-start = (bf16[1,128,2304]{2,1,0:T(8,128)(2,1)S(1)}, bf16[1,128,2304]{2,1,0:T(8,128)(2,1)}, u32[]{:S(2)}) copy-start(bf16[1,128,2304]{2,1,0:T(8,128)(2,1)} %param.9) | copy-start | bytes 1769476
  7.2 12.8 %copy-start.16 = (bf16[1,128,1024]{2,1,0:T(8,128)(2,1)S(1)}, bf16[1,128,1024]{2,1,0:T(8,128)(2,1)}, u32[]{:S(2)}) copy-start(bf16[1,128,1024]{2,1,0:T(8,128)(2,1)} %param.11) | copy-start | bytes 786436
  7.2 12.0 %copy-start.15 = (bf16[1,128,1024]{2,1,0:T(8,128)(2,1)S(1)}, bf16[1,128,1024]{2,1,0:T(8,128)(2,1)}, u32[]{:S(2)}) copy-start(bf16[1,128,1024]{2,1,0:T(8,128)(2,1)} %param.12) | copy-start | bytes 786436
  7.2 7.0 %copy-start.31 = (s32[64]{0:T(128)S(1)}, s32[64]{0:T(128)}, u32[]{:S(2)}) copy-start(s32[64]{0:T(128)} %param.16) | copy-start | bytes 772
  7.2 10.1 %copy-start.34 = (s32[1,4]{1,0:T(1,128)S(1)}, s32[1,4]{1,0:T(1,128)}, u32[]{:S(2)}) copy-start(s32[1,4]{1,0:T(1,128)} %param.17) | copy-start | bytes 52
  7.2 13.0 %copy-start.18 = (bf16[1,128,2048]{2,1,0:T(8,128)(2,1)S(1)}, bf16[1,128,2048]{2,1,0:T(8,128)(2,1)}, u32[]{:S(2)}) copy-start(bf16[1,128,2048]{2,1,0:T(8,128)(2,1)} %param.14) | copy-start | bytes 1572868
  7.2 364.1 %reduce-scatter.4.cloned.1.call-start = ((), (), s32[]{:S(2)}) async-start(), calls=%async_computation.1 | async-start | bytes 19464192
  10.5 10.7 %copy-start.19 = (bf16[1,128,2048]{2,1,0:T(8,128)(2,1)S(1)}, bf16[1,128,2048]{2,1,0:T(8,128)(2,1)}, u32[]{:S(2)}) copy-start(bf16[1,128,2048]{2,1,0:T(8,128)(2,1)} %param.10) | copy-start | bytes 1572868
  10.5 35.0 %collective-permute-start.2 = (bf16[2,128,1024]{1,2,0:T(8,128)(2,1)}, bf16[2,128,1024]{1,2,0:T(8,128)(2,1)}, u32[]{:S(2)}, u32[]{:S(2)}) collective-permute-start(bf16[2,128,1024]{1,2,0:T(8,128)(2,1)} %pad_maximum_fusion.1), channel_id=1, source_target_pairs={{0,32},{32,64},{64,96},{96,128},{128,160},{160,192},{192,224},{224... | collective-permute-start | bytes 1572872 | tf_op jit(solution)/shard_map/ppermute | solution.py:17
  12.5 27.6 %collective-permute-start = (bf16[2,128,1024]{1,2,0:T(8,128)(2,1)}, bf16[2,128,1024]{1,2,0:T(8,128)(2,1)}, u32[]{:S(2)}, u32[]{:S(2)}) collective-permute-start(bf16[2,128,1024]{1,2,0:T(8,128)(2,1)} %pad_maximum_fusion.1), channel_id=1, source_target_pairs={{0,4},{4,8},{8,12},{12,16},{16,20},{20,24},{24,28},{28,0},{1,5},{5... | collective-permute-start | bytes 1572872 | tf_op jit(solution)/shard_map/ppermute | solution.py:17
  17.3 4.5 %copy-start.33 = (s32[128]{0:T(128)}, s32[128]{0:T(128)S(1)}, u32[]{:S(2)}) copy-start(s32[128]{0:T(128)S(1)} %iota_add_fusion.2) | copy-start | bytes 1540
  17.5 4.3 %copy-start.32 = (s32[128]{0:T(128)}, s32[128]{0:T(128)S(1)}, u32[]{:S(2)}) copy-start(s32[128]{0:T(128)S(1)} %get-tuple-element.34) | copy-start | bytes 1540
  38.9 3.4 copy-start.24
  50.5 2.5 copy-start.28
  50.5 2.5 copy-start.29
  53.0 3.7 copy-start.3
  53.6 15.9 %collective-permute-start.1 = (bf16[2,128,1024]{1,2,0:T(8,128)(2,1)}, bf16[2,128,1024]{1,2,0:T(8,128)(2,1)}, u32[]{:S(2)}, u32[]{:S(2)}) collective-permute-start(bf16[2,128,1024]{1,2,0:T(8,128)(2,1)} %collective-permute-done), channel_id=1, source_target_pairs={{0,4},{4,8},{8,12},{12,16},{16,20},{20,24},{24,28},{28,0},{1,5},{5... | collective-permute-start | bytes 1572872 | tf_op jit(solution)/shard_map/ppermute | solution.py:17
  58.0 13.6 %copy-start.26 = (f32[1,16,128]{2,1,0:T(8,128)S(1)}, f32[1,16,128]{2,1,0:T(8,128)}, u32[]{:S(2)}) copy-start(f32[1,16,128]{2,1,0:T(8,128)} %param.15) | copy-start | bytes 24580
  58.0 13.6 %copy-start.27 = (pred[128,128]{0,1:T(8,128)(4,1)S(1)}, pred[128,128]{0,1:T(8,128)(4,1)}, u32[]{:S(2)}) copy-start(pred[128,128]{0,1:T(8,128)(4,1)} %get-tuple-element.26) | copy-start | bytes 49156
  59.8 35.1 %collective-permute-start.5 = (bf16[2,128,1024]{2,1,0:T(8,128)(2,1)}, bf16[2,128,1024]{2,1,0:T(8,128)(2,1)}, u32[]{:S(2)}, u32[]{:S(2)}) collective-permute-start(bf16[2,128,1024]{2,1,0:T(8,128)(2,1)} %pad_maximum_fusion.4), channel_id=1, source_target_pairs={{0,224},{32,0},{64,32},{96,64},{128,96},{160,128},{192,160},{224,1... | collective-permute-start | bytes 1572872 | tf_op jit(solution)/shard_map/ppermute | solution.py:17
  71.3 3.2 copy-start.30
  76.0 4.4 %copy-start.2 = (f32[128,8,2,128]{0,3,2,1:T(8,128)S(1)}, f32[128,8,2,128]{0,3,2,1:T(8,128)}, u32[]{:S(2)}) copy-start(f32[128,8,2,128]{0,3,2,1:T(8,128)} %convolution_bitcast_fusion) | copy-start | bytes 3145732
  76.1 4.4 %copy-start.4 = (bf16[8,2,128,128]{2,3,1,0:T(8,128)(2,1)S(1)}, bf16[8,2,128,128]{2,3,1,0:T(8,128)(2,1)}, u32[]{:S(2)}) copy-start(bf16[8,2,128,128]{2,3,1,0:T(8,128)(2,1)} %fusion.25) | copy-start | bytes 1572868
  78.2 2.6 copy-start.12
  79.3 11.9 %collective-permute-start.3 = (bf16[2,128,1024]{2,1,0:T(8,128)(2,1)S(1)}, bf16[2,128,1024]{2,1,0:T(8,128)(2,1)S(1)}, u32[]{:S(2)}, u32[]{:S(2)}) collective-permute-start(bf16[2,128,1024]{2,1,0:T(8,128)(2,1)S(1)} %pad_maximum_fusion.3), channel_id=1, source_target_pairs={{0,28},{4,0},{8,4},{12,8},{16,12},{20,16},{24,20},{28,24},{1,29},{... | collective-permute-start | bytes 1572872 | tf_op jit(solution)/shard_map/ppermute | solution.py:17
  80.8 10.4 %copy-start.7 = (f32[1,128,1024]{2,1,0:T(8,128)S(1)}, f32[1,128,1024]{2,1,0:T(8,128)}, u32[]{:S(2)}) copy-start(f32[1,128,1024]{2,1,0:T(8,128)} %copy.196) | copy-start | bytes 1572868
  80.8 10.4 %copy-start.10 = (f32[1,128,1024]{2,1,0:T(8,128)S(1)}, f32[1,128,1024]{2,1,0:T(8,128)}, u32[]{:S(2)}) copy-start(f32[1,128,1024]{2,1,0:T(8,128)} %copy.195) | copy-start | bytes 1572868
  80.8 13.4 %copy-start.9 = (bf16[8,2,128,128]{2,3,1,0:T(8,128)(2,1)S(1)}, bf16[8,2,128,128]{2,3,1,0:T(8,128)(2,1)}, u32[]{:S(2)}) copy-start(bf16[8,2,128,128]{2,3,1,0:T(8,128)(2,1)} %copy-done.8) | copy-start | bytes 1572868
  92.2 11.2 %collective-permute-start.4 = (bf16[2,128,1024]{2,1,0:T(8,128)(2,1)}, bf16[2,128,1024]{2,1,0:T(8,128)(2,1)S(1)}, u32[]{:S(2)}, u32[]{:S(2)}) collective-permute-start(bf16[2,128,1024]{2,1,0:T(8,128)(2,1)} %fusion.32), channel_id=1, source_target_pairs={{0,28},{4,0},{8,4},{12,8},{16,12},{20,16},{24,20},{28,24},{1,29},{... | collective-permute-start | bytes 1572872 | tf_op jit(solution)/shard_map/ppermute | solution.py:17
  94.5 8.8 %copy-start.5 = (f32[1,128,1024]{2,1,0:T(8,128)S(1)}, f32[1,128,1024]{2,1,0:T(8,128)}, u32[]{:S(2)}) copy-start(f32[1,128,1024]{2,1,0:T(8,128)} %copy.202) | copy-start | bytes 1572868
  94.5 8.8 %copy-start.6 = (f32[1,128,1024]{2,1,0:T(8,128)S(1)}, f32[1,128,1024]{2,1,0:T(8,128)}, u32[]{:S(2)}) copy-start(f32[1,128,1024]{2,1,0:T(8,128)} %copy.201) | copy-start | bytes 1572868
  138.7 235.5 %copy-start.1 = (bf16[1,128,2304]{2,1,0:T(8,128)(2,1)S(1)}, bf16[1,128,2304]{2,1,0:T(8,128)(2,1)}, u32[]{:S(2)}) copy-start(bf16[1,128,2304]{2,1,0:T(8,128)(2,1)} %param.9) | copy-start | bytes 1769476
  (10 other events, 15.3 us)
Sparse Core Ops, SparseCore 0:
  138.8 232.5 reduce-scatter.3
where the time goes:
time: 385 us; the launch traced here: 381 us
  waiting for transfers between devices  257 us (67%)
  local copies, waits for them, and re-layouts  56.5 us (15%)
  matrix products  25.9 us (7%)
  between operations  17.1 us (4%)
  other arithmetic  12.8 us (3%)
  starting transfers between devices  11.3 us (3%)
    unnamed x2, waiting for transfers between devices  232 us
    unnamed x80, local copies, waits for them, and re-layouts  31.8 us
    ppermute x6, waiting for transfers between devices, from_behind(): lax.ppermute(x, axis, [(i, (i + by) % devices) for i in range(devices)])  25.7 us
    ppermute x6, starting transfers between devices, from_behind(): lax.ppermute(x, axis, [(i, (i + by) % devices) for i in range(devices)])  11.3 us
    another operation x8, local copies, waits for them, and re-layouts, attend(): return (dq, jnp.stack([dk, dv]))  10.7 us
    dot_general x1, matrix products, local(): lax.dot_general(x_rows, all_grads, (((0,), (0,)), ((), ())), preferred_el...  9.24 us
  transfers between devices with their start and end apart: 7, of which 4 were waited for; matrix products, arithmetic and copies ran while one was open for 12% of the time, Pallas kernels for 0%

commit v1 on v0

v1 whole, which is shorter than its diff:
```python
import functools

import jax
import jax.numpy as jnp
import numpy as np
from jax import lax
from jax.experimental import pallas as pl
from jax.experimental.pallas import tpu as pltpu
from jax.sharding import PartitionSpec as P

MESH = pl.DeviceIdType.MESH
F32 = jnp.float32
BF16 = jnp.bfloat16

HQ = 16
HK = 8
HD = 128
TOK = 128
D = 2304
COLS = 4096
RING = 8
QUAD = 4
GROUPS = 4
ROWS = D // RING // 2
HALF = 512
DEAD = -1e30

CHUNKS = ((0, 512), (2048, 3072), (1024, 1536), (2560, 3584))
DQ0, DKV0, DQ1, DKV1 = 0, 1, 2, 3


def nt(a, b):
    return lax.dot_general(a, b, (((1,), (1,)), ((), ())), preferred_element_type=F32)


def tn(a, b):
    return lax.dot_general(a, b, (((0,), (0,)), ((), ())), preferred_element_type=F32)


def nn(a, b):
    return jnp.dot(a, b, preferred_element_type=F32)


def kernel(
    hid, q, k, v, fo, do, lse, order, lengths, inv,
    gout, wout,
    kvr, bias, cosf, sinf, delta, dq_acc, home, one_part,
    two_send, two_recv, car_send, car_recv, pri_send, pri_recv,
    g, xt, xt_core, xt_far, gq, part, rs_send, rs_recv, fin, fin_send, fin_recv,
    kv_s, kv_r, ret_s, ret_r, xt_s, xt_r, gx_s, gx_r, rs_ss, rs_rs, fin_s, fin_r,
):
    z = lax.axis_index("inner")
    oo = lax.axis_index("outer")
    f = lax.axis_index("fsdp")
    xh = f // 2
    c = f % 2
    up = {"inner": (z + 1) % RING}
    down = {"inner": (z + RING - 1) % RING}
    n_outer = lax.axis_size("outer")
    nxt = {"outer": (oo + 1) % n_outer}
    prv = {"outer": (oo + n_outer - 1) % n_outer}
    core = {"fsdp": xh * 2 + 1 - c}
    far = {"fsdp": (1 - xh) * 2 + c}

    sends = []

    def send(src, dst, ss, rs, to):
        cp = pltpu.make_async_remote_copy(
            src_ref=src, dst_ref=dst, send_sem=ss, recv_sem=rs, device_id=to, device_id_type=MESH
        )
        cp.start()
        sends.append(cp)
        return cp

    barrier = pltpu.get_barrier_semaphore()
    for to in (up, down, nxt, prv, core, far):
        pl.semaphore_signal(barrier, inc=1, device_id=to, device_id_type=MESH)
    pl.semaphore_wait(barrier, 6)

    cp_one, cp_two, cp_pri = {}, {}, {}
    for gi in range(GROUPS):
        cols = pl.ds(gi * 256, 256)
        for j, ref in enumerate((k, v)):
            cp_one[gi, j] = send(
                ref.at[:, cols], kvr.at[0, j, :, cols], kv_s.at[0, gi, j], kv_r.at[0, gi, j], up
            )
        for j, ref in enumerate((k, v)):
            cp_pri[gi, j] = send(
                ref.at[:, cols], kvr.at[2, j, :, cols], kv_s.at[2, gi, j], kv_r.at[2, gi, j], nxt
            )

    def forward(gi):
        cols = pl.ds(gi * 256, 256)
        for j in range(2):
            cp_one[gi, j].wait_recv()
            cp_two[gi, j] = send(
                kvr.at[0, j, :, cols], kvr.at[1, j, :, cols], kv_s.at[1, gi, j], kv_r.at[1, gi, j], up
            )

    turned = hid[...].T
    for i in range(2 * RING):
        xt[i // 2, i % 2] = turned[i * ROWS : (i + 1) * ROWS]
    cp_xc = send(xt, xt_core, xt_s.at[0], xt_r.at[0], core)
    cp_xf = send(xt.at[:, 1 - xh], xt_far.at[0], xt_s.at[1], xt_r.at[1], far)

    rows_i = lax.broadcasted_iota(jnp.int32, (TOK, TOK), 0)
    cols_i = lax.broadcasted_iota(jnp.int32, (TOK, TOK), 1)
    starts = [jnp.int32(0)]
    for i in range(3):
        starts.append(starts[-1] + lengths[0, i])

    def doc_of(pos):
        total = jnp.zeros(pos.shape, jnp.int32)
        for s in starts:
            total = total + (pos >= s).astype(jnp.int32)
        return total

    def block(outer_pos, inner_pos):
        return order[(outer_pos % n_outer) * RING + inner_pos % RING] * TOK

    qpos = block(oo, z) + cols_i
    qdoc = doc_of(qpos)
    slots = ((oo, z), (oo, z + RING - 1), (oo, z + RING - 2), (oo + n_outer - 1, z))
    for i, (a, b) in enumerate((slots[0], slots[1], slots[3], slots[2])):
        kpos = block(a, b) + rows_i
        live = (kpos <= qpos) & (doc_of(kpos) == qdoc)
        bias[i] = jnp.where(live, F32(0.0), F32(DEAD))
    angle = (block(oo, z) + rows_i).astype(F32) * inv[0:1, :]
    cosf[...] = jnp.cos(angle)
    sine = jnp.sin(angle)
    sinf[...] = jnp.where(cols_i < HD // 2, sine, -sine)

    def unrotate(grad):
        return grad * cosf[...] + pltpu.roll(grad, HD // 2, 1) * sinf[...]

    ones = jnp.ones((8, HD), BF16)
    for h in range(HQ):
        cols = slice(h * HD, (h + 1) * HD)
        prod = do[:, cols].astype(F32) * fo[:, cols].astype(F32)
        hi = prod.astype(BF16)
        lo = (prod - hi.astype(F32)).astype(BF16)
        delta[h : h + 1] = (nt(ones, hi) + nt(ones, lo))[0:1]

    cp_xc.wait_recv()
    cp_xd = send(xt_core.at[:, 1 - xh], xt_far.at[1], xt_s.at[2], xt_r.at[2], far)

    def attend(h, kk, vv, bb):
        a, b = slice(2 * h * HD, (2 * h + 1) * HD), slice((2 * h + 1) * HD, (2 * h + 2) * HD)
        qs = jnp.concatenate([q[:, a], q[:, b]], axis=0)
        dos = jnp.concatenate([do[:, a], do[:, b]], axis=0)
        lse_h = jnp.concatenate([lse[2 * h : 2 * h + 1], lse[2 * h + 1 : 2 * h + 2]], axis=1)
        delta_h = jnp.concatenate([delta[2 * h : 2 * h + 1], delta[2 * h + 1 : 2 * h + 2]], axis=1)
        capped = jnp.tanh(nt(kk, qs) * F32(1.0 / 600.0))
        prob = jnp.exp(F32(50.0) * capped - lse_h + jnp.concatenate([bb, bb], axis=1))
        dprob = nt(vv, dos)
        ds = (prob * (dprob - delta_h) * (F32(1.0 / 12.0) - F32(1.0 / 12.0) * (capped * capped))).astype(BF16)
        return tn(ds, kk), nn(ds, qs), nn(prob.astype(BF16), dos)

    def first(gi):
        for hh in range(2):
            h = gi * 2 + hh
            cols = slice(h * HD, (h + 1) * HD)
            kk = jnp.concatenate([k[:, cols], kvr[0, 0, :, cols], kvr[2, 0, :, cols]], axis=0)
            vv = jnp.concatenate([v[:, cols], kvr[0, 1, :, cols], kvr[2, 1, :, cols]], axis=0)
            dq, dk, dv = attend(h, kk, vv, bias[0:3].reshape(3 * TOK, TOK))
            dq_acc[h] = dq
            for j, val in enumerate((dk, dv)):
                home[gi, hh, j] = val[0:TOK]
                one_part[gi, hh, j] = val[TOK : 2 * TOK]
                pri_send[gi, hh, j] = val[2 * TOK : 3 * TOK].astype(BF16)

    def second(gi):
        for hh in range(2):
            h = gi * 2 + hh
            cols = slice(h * HD, (h + 1) * HD)
            dq, dk, dv = attend(h, kvr[1, 0, :, cols], kvr[1, 1, :, cols], bias[3])
            for j, val in enumerate((dk, dv)):
                two_send[gi, hh, j] = val.astype(BF16)
            total = dq_acc[h] + dq
            for i in range(2):
                g[:, (2 * h + i) * HD : (2 * h + i + 1) * HD] = unrotate(total[i * TOK : (i + 1) * TOK]).astype(BF16)

    cp_ret = {}

    def do_first(gi):
        forward(gi)
        for j in range(2):
            cp_pri[gi, j].wait_recv()
        first(gi)
        cp_ret["pri", gi] = send(pri_send.at[gi], pri_recv.at[gi], ret_s.at[0, gi], ret_r.at[0, gi], prv)

    def do_second(gi):
        for j in range(2):
            cp_two[gi, j].wait_recv()
        second(gi)
        cp_ret["two", gi] = send(two_send.at[gi], two_recv.at[gi], ret_s.at[1, gi], ret_r.at[1, gi], down)

    def carry(gi):
        cp_ret["two", gi].wait_recv()
        car_send[gi] = (two_recv[gi].astype(F32) + one_part[gi]).astype(BF16)
        cp_ret["car", gi] = send(car_send.at[gi], car_recv.at[gi], ret_s.at[2, gi], ret_r.at[2, gi], down)

    def settle(gi):
        cp_ret["car", gi].wait_recv()
        cp_ret["pri", gi].wait_recv()
        for hh in range(2):
            h = gi * 2 + hh
            dk, dv = [
                home[gi, hh, j] + car_recv[gi, hh, j].astype(F32) + pri_recv[gi, hh, j].astype(F32)
                for j in range(2)
            ]
            at = HQ * HD + h * HD
            g[:, at : at + HD] = unrotate(dk).astype(BF16)
            at = (HQ + HK) * HD + h * HD
            g[:, at : at + HD] = dv.astype(BF16)

    cp_gx = {}

    def base(ch, who):
        lo, hi = CHUNKS[ch]
        return pl.ds(pl.multiple_of(lo + who * (hi - lo), HALF), HALF)

    def swap(ch):
        mine = g.at[:, base(ch, c)]
        cp_gx[ch, 0] = send(g.at[:, base(ch, 1 - c)], gq.at[ch, 1], gx_s.at[ch, 0], gx_r.at[ch, 0], core)
        cp_gx[ch, 1] = send(mine, gq.at[ch, 2], gx_s.at[ch, 1], gx_r.at[ch, 1], far)
        gq[ch, 0] = mine[...]

    def swap_on(ch):
        cp_gx[ch, 0].wait_recv()
        cp_gx[ch, 2] = send(gq.at[ch, 1], gq.at[ch, 3], gx_s.at[ch, 2], gx_r.at[ch, 2], far)

    chains = ((0, 1, 4), (0, -1, 3), (1, -1, 4), (1, 1, 3))
    cp_rs = {}

    def term(ch, chain, step):
        half, way, hops = chains[chain]
        at = (z + 2 * RING + way * (hops - step)) % RING
        return part[ch, at, :, half * 256 : (half + 1) * 256]

    def hop(ch, chain, step, val):
        rs_send[ch, chain, step] = val.astype(BF16)
        cp_rs[ch, chain, step] = send(
            rs_send.at[ch, chain, step], rs_recv.at[ch, chain, step],
            rs_ss.at[ch, chain, step], rs_rs.at[ch, chain, step],
            up if chains[chain][1] > 0 else down,
        )

    def multiply(ch):
        cp_gx[ch, 1].wait_recv()
        cp_gx[ch, 2].wait_recv()
        for half in range(2):
            gs = gq[ch, :, :, half * 256 : (half + 1) * 256].reshape(QUAD * TOK, 256)
            for piece in range(2):
                at = slice(piece * 4, piece * 4 + 4)
                xs = jnp.concatenate(
                    [xt_mine[at], xt_mate[at], xt_far[0, at], xt_far[1, at]], axis=-1
                ).reshape(4 * ROWS, QUAD * TOK)
                part[ch, at, :, half * 256 : (half + 1) * 256] = nn(xs, gs).reshape(4, ROWS, 256)
        for chain in range(4):
            hop(ch, chain, 0, term(ch, chain, 0))

    def step(ch, s):
        for chain in range(4):
            if s < chains[chain][2]:
                cp_rs[ch, chain, s - 1].wait_recv()
                hop(ch, chain, s, rs_recv[ch, chain, s - 1].astype(F32) + term(ch, chain, s))

    def finish(ch):
        for half in range(2):
            val = part[ch, z, :, half * 256 : (half + 1) * 256]
            for chain in range(4):
                if chains[chain][0] == half:
                    last = chains[chain][2] - 1
                    cp_rs[ch, chain, last].wait_recv()
                    val = val + rs_recv[ch, chain, last].astype(F32)
            fin[ch, 0, :, half * 256 : (half + 1) * 256] = val[0 : ROWS // 2]
            fin[ch, 1, :, half * 256 : (half + 1) * 256] = val[ROWS // 2 :]
        fin_send[ch] = fin[ch, 1 - c].astype(BF16)
        cp_gx[ch, "fin"] = send(fin_send.at[ch], fin_recv.at[ch], fin_s.at[ch], fin_r.at[ch], core)
        wout[:, base(ch, c)] = fin[ch, c].astype(BF16)

    def last(ch):
        cp_gx[ch, "fin"].wait_recv()
        wout[:, base(ch, 1 - c)] = fin_recv[ch]

    xt_mine = xt.at[:, xh]
    xt_mate = xt_core.at[:, xh]

    for gi in range(GROUPS):
        do_first(gi)
    do_second(0)
    do_second(1)
    swap(DQ0)
    carry(0)
    do_second(2)
    carry(1)
    swap_on(DQ0)
    do_second(3)
    swap(DQ1)
    settle(0)
    settle(1)
    swap(DKV0)
    carry(2)
    swap_on(DQ1)
    carry(3)
    cp_xf.wait_recv()
    cp_xd.wait_recv()
    multiply(DQ0)
    swap_on(DKV0)
    settle(2)
    settle(3)
    swap(DKV1)
    step(DQ0, 1)
    multiply(DQ1)
    swap_on(DKV1)
    multiply(DKV0)
    step(DQ0, 2)
    step(DQ1, 1)
    step(DKV0, 1)
    multiply(DKV1)
    step(DQ0, 3)
    step(DQ1, 2)
    step(DKV0, 2)
    step(DKV1, 1)
    finish(DQ0)
    step(DQ1, 3)
    step(DKV0, 3)
    step(DKV1, 2)
    gout[...] = g[...]
    finish(DQ1)
    finish(DKV0)
    step(DKV1, 3)
    last(DQ0)
    last(DQ1)
    last(DKV0)
    finish(DKV1)
    last(DKV1)
    for cp in sends:
        cp.wait_send()


def local(hidden_in, queries, keys, values, fwd_out, out_grad, lse, block_order, doc_lengths):
    freq = 10000.0 ** (-2.0 * np.arange(HD // 2, dtype=np.float32) / HD)
    inv = jnp.asarray(np.broadcast_to(np.concatenate([freq, freq])[None, :], (8, HD)).astype(np.float32))
    vm = pl.BlockSpec(memory_space=pltpu.VMEM)
    sm = pl.BlockSpec(memory_space=pltpu.SMEM)
    ret = pltpu.VMEM((GROUPS, 2, 2, TOK, HD), BF16)
    dma = pltpu.SemaphoreType.DMA
    qkv, weights = pl.pallas_call(
        kernel,
        out_shape=(
            jax.ShapeDtypeStruct((TOK, COLS), BF16),
            jax.ShapeDtypeStruct((ROWS // 2, COLS), BF16),
        ),
        in_specs=[vm] * 7 + [sm, sm, vm],
        out_specs=(vm, vm),
        scratch_shapes=[
            pltpu.VMEM((3, 2, TOK, HK * HD), BF16),
            pltpu.VMEM((4, TOK, TOK), F32),
            pltpu.VMEM((TOK, HD), F32),
            pltpu.VMEM((TOK, HD), F32),
            pltpu.VMEM((HQ, TOK), F32),
            pltpu.VMEM((HK, 2 * TOK, HD), F32),
            pltpu.VMEM((GROUPS, 2, 2, TOK, HD), F32),
            pltpu.VMEM((GROUPS, 2, 2, TOK, HD), F32),
            ret, ret, ret, ret, ret, ret,
            pltpu.VMEM((TOK, COLS), BF16),
            pltpu.VMEM((RING, 2, ROWS, TOK), BF16),
            pltpu.VMEM((RING, 2, ROWS, TOK), BF16),
            pltpu.VMEM((2, RING, ROWS, TOK), BF16),
            pltpu.VMEM((4, QUAD, TOK, HALF), BF16),
            pltpu.VMEM((4, RING, ROWS, HALF), F32),
            pltpu.VMEM((4, 4, 4, ROWS, 256), BF16),
            pltpu.VMEM((4, 4, 4, ROWS, 256), BF16),
            pltpu.VMEM((4, 2, ROWS // 2, HALF), F32),
            pltpu.VMEM((4, ROWS // 2, HALF), BF16),
            pltpu.VMEM((4, ROWS // 2, HALF), BF16),
            dma((3, GROUPS, 2)), dma((3, GROUPS, 2)),
            dma((3, GROUPS)), dma((3, GROUPS)),
            dma((3,)), dma((3,)),
            dma((4, 3)), dma((4, 3)),
            dma((4, 4, 4)), dma((4, 4, 4)),
            dma((4,)), dma((4,)),
        ],
        compiler_params=pltpu.CompilerParams(
            collective_id=0, has_side_effects=True, vmem_limit_bytes=58 * 1024 * 1024
        ),
        cost_estimate=pl.CostEstimate(flops=4 * 10**9, bytes_accessed=6 * 10**6, transcendentals=2 * 10**6),
    )(
        hidden_in[0], queries[0], keys[0], values[0], fwd_out[0], out_grad[0], lse[0],
        block_order, doc_lengths, inv,
    )
    return (qkv[None], weights[None])


def solution(mesh):
    tokens = P("fsdp", ("outer", "inner"), None)
    in_specs = (tokens,) * 6 + (P("fsdp", None, ("outer", "inner")), P(), P("fsdp", None))
    out_specs = (tokens, P("outer", ("inner", "fsdp"), None))
    return jax.shard_map(local, mesh=mesh, in_specs=in_specs, out_specs=out_specs, check_vma=False)
```

time: 385 us -> 115 us (0.30)
  waiting for transfers between devices: 257 us -> 0 us
  Pallas kernels: 0 us -> 111 us
  local copies, waits for them, and re-layouts: 56.5 us -> 3.17 us
  matrix products: 25.9 us -> 0 us
  between operations: 17.1 us -> 0.65 us
  other arithmetic: 12.8 us -> 0 us
  starting transfers between devices: 11.3 us -> 0 us
    unnamed x2 -> x0, waiting for transfers between devices: 232 us -> none
    pallas_call x0 -> x1, Pallas kernels: none -> 111 us  [local(): pl.pallas_call(kernel, out_shape=(jax.ShapeDtypeStruct((TOK, COLS), BF16)...]
    unnamed x80 -> x4, local copies, waits for them, and re-layouts: 31.8 us -> 3.17 us
    dot_general x21 -> x0, matrix products: 25.9 us -> none  [the longest x1 9.24 us: local(): lax.dot_general(x_rows, all_grads, (((0,), (0,)), ((), ())), preferred_el...]
    ppermute x6 -> x0, waiting for transfers between devices: 25.7 us -> none  [from_behind(): lax.ppermute(x, axis, [(i, (i + by) % devices) for i in range(devices)])]
    another operation x12 -> x0, local copies, waits for them, and re-layouts: 12.1 us -> none  [the longest x8 10.7 us: attend(): return (dq, jnp.stack([dk, dv]))]
    ppermute x6 -> x0, starting transfers between devices: 11.3 us -> none  [from_behind(): lax.ppermute(x, axis, [(i, (i + by) % devices) for i in range(devices)])]
    slice x3 -> x0, local copies, waits for them, and re-layouts: 5.31 us -> none  [attend(): vb = kv_pair[1].reshape(tok, kv_heads, head_size)]
  transfers between devices with their start and end apart: 7 -> 0, of which waited for: 4 -> 0; matrix products, arithmetic and copies ran while one was open for 12% -> 0% of each run, Pallas kernels for 0% -> 0%
where the time goes in v1:
time: 115 us
  Pallas kernels  111 us (97%)
  local copies, waits for them, and re-layouts  3.17 us (3%)
    pallas_call x1, Pallas kernels, local(): pl.pallas_call(kernel, out_shape=(jax.ShapeDtypeStruct((TOK, COLS), BF16)...  111 us
    unnamed x4, local copies, waits for them, and re-layouts  3.17 us

profile of v1, /device:TPU:1, one launch (start us, length us, event | category | flops | bytes accessed | tf_op | source)
XLA Modules:
  0.0 114.7 jit_solution(14093216647209943777)
XLA Ops:
  0.6 110.9 %shard_map.113 = (bf16[128,4096]{1,0:T(8,128)(2,1)}, bf16[72,4096]{1,0:T(8,128)(2,1)}) custom-call(bf16[128,2304]{1,0:T(8,128)(2,1)} %bitcast.11, bf16[128,2048]{1,0:T(8,128)(2,1)} %bitcast.12, bf16[128,1024]{1,0:T(8,128)(2,1)} %bitcast.15, bf16[128,1024]{1,0:T(8,128)(2,1)} %bitcast.16, bf16[128,2048]{1,0:T(8,128)(2,1)} %bitcast.13, ...), custom_call_target="tpu_custom_call" | custom-call | flops 4000000000 | bytes 6000000 | tf_op jit(solution)/shard_map/pallas_call | solution.py:350
  111.6 0.0 copy-start
  111.6 2.3 %copy.14 = bf16[1,128,4096]{2,1,0:T(8,128)(2,1)} copy(bf16[1,128,4096]{2,1,0:T(8,128)(2,1)} %bitcast.9) | data formatting | bytes 2097152
  113.9 0.0 copy-done
  113.9 0.8 copy.15
Async XLA Ops:
  111.6 2.4 %copy-start = (bf16[72,4096]{1,0:T(8,128)(2,1)S(1)}, bf16[72,4096]{1,0:T(8,128)(2,1)}, u32[]{:S(2)}) copy-start(bf16[72,4096]{1,0:T(8,128)(2,1)} %get-tuple-element.5) | copy-start | bytes 1769476

commit v2 on v1

v2 whole, which is shorter than its diff:
```python
import functools

import jax
import jax.numpy as jnp
import numpy as np
from jax import lax
from jax.experimental import pallas as pl
from jax.experimental.pallas import tpu as pltpu
from jax.sharding import PartitionSpec as P

MESH = pl.DeviceIdType.MESH
F32 = jnp.float32
BF16 = jnp.bfloat16

HQ = 16
HK = 8
HD = 128
TOK = 128
D = 2304
COLS = 4096
RING = 8
QUAD = 4
GROUPS = 4
ROWS = D // RING // 2
HALF = 256
DEAD = -1e30

CHUNKS = tuple((512 * i, 512 * i + 256) for i in range(4)) + tuple(
    (2048 + 256 * i, 3072 + 256 * i) for i in range(4)
)
LONG_UP = ((1, 4), (-1, 3))
LONG_DOWN = ((1, 3), (-1, 4))
CHAINS = (LONG_UP, LONG_DOWN, LONG_UP, LONG_UP, LONG_DOWN, LONG_UP, LONG_UP, LONG_UP)
ORDER = (
    ("pri", 0), ("pri", 2), ("one", 2), ("turn",), ("prep",), ("one", 0), ("fwd", 2), ("first", 2), ("fwd", 0),
    ("first", 0), ("second", 2), ("swap", 2), ("relay", 2), ("one", 1), ("pri", 1), ("second", 0), ("swap", 0),
    ("xon",), ("relay", 0), ("carry", 2), ("xready",), ("fwd", 1), ("first", 1), ("one", 3), ("carry", 0), ("pri", 3),
    ("mult", 2), ("settle", 2), ("swap", 6), ("second", 1), ("relay", 6), ("swap", 1), ("relay", 1), ("fwd", 3),
    ("first", 3), ("settle", 0), ("swap", 4), ("step", 2, 1), ("relay", 4), ("mult", 0), ("carry", 1), ("second", 3),
    ("swap", 3), ("step", 2, 2), ("step", 0, 1), ("relay", 3), ("settle", 1), ("swap", 5), ("step", 2, 3),
    ("mult", 6), ("relay", 5), ("carry", 3), ("mult", 1), ("finish", 2), ("last", 2), ("step", 0, 2), ("mult", 4),
    ("step", 6, 1), ("step", 0, 3), ("settle", 3), ("swap", 7), ("relay", 7), ("step", 1, 1), ("mult", 3),
    ("finish", 0), ("step", 4, 1), ("mult", 5), ("last", 0), ("step", 6, 2), ("mult", 7), ("step", 1, 2),
    ("step", 3, 1), ("step", 4, 2), ("step", 6, 3), ("step", 5, 1), ("step", 7, 1), ("step", 1, 3), ("step", 3, 2),
    ("finish", 6), ("step", 4, 3), ("last", 6), ("step", 5, 2), ("step", 7, 2), ("step", 3, 3), ("finish", 1),
    ("last", 1), ("step", 5, 3), ("step", 7, 3), ("finish", 4), ("last", 4), ("finish", 3), ("last", 3),
    ("finish", 5), ("last", 5), ("finish", 7), ("last", 7),
)


def nt(a, b):
    return lax.dot_general(a, b, (((1,), (1,)), ((), ())), preferred_element_type=F32)


def tn(a, b):
    return lax.dot_general(a, b, (((0,), (0,)), ((), ())), preferred_element_type=F32)


def nn(a, b):
    return jnp.dot(a, b, preferred_element_type=F32)


def kernel(
    hid_hbm, q_hbm, k_hbm, v_hbm, fo_hbm, do_hbm, lse, order, lengths, inv,
    gout, wout,
    hid, q, k, v, fo, do,
    kvr, bias, cosf, sinf, delta, dq_acc, home, one_part,
    two_send, two_recv, car_send, car_recv, pri_send, pri_recv,
    g, xt, xt_core, xt_far, gq, part, rs_send, rs_recv, fin, fin_send, fin_recv,
    in_s, kv_s, kv_r, ret_s, ret_r, xt_s, xt_r, gx_s, gx_r, rs_ss, rs_rs, fin_s, fin_r,
):
    z = lax.axis_index("inner")
    oo = lax.axis_index("outer")
    f = lax.axis_index("fsdp")
    n_outer = lax.axis_size("outer")
    xh = f // 2
    c = f % 2
    up = {"inner": (z + 1) % RING}
    down = {"inner": (z + RING - 1) % RING}
    nxt = {"outer": (oo + 1) % n_outer}
    prv = {"outer": (oo + n_outer - 1) % n_outer}
    core = {"fsdp": xh * 2 + 1 - c}
    far = {"fsdp": (1 - xh) * 2 + c}

    sends = []
    cps = {}

    def send(name, src, dst, ss, rs, to):
        cp = pltpu.make_async_remote_copy(
            src_ref=src, dst_ref=dst, send_sem=ss, recv_sem=rs, device_id=to, device_id_type=MESH
        )
        cp.start()
        sends.append(cp)
        cps[name] = cp

    barrier = pltpu.get_barrier_semaphore()
    for to in (up, down, nxt, prv, core, far):
        pl.semaphore_signal(barrier, inc=1, device_id=to, device_id_type=MESH)
    loads = {}
    for i, (name, src, dst) in enumerate((
        ("k", k_hbm, k), ("v", v_hbm, v), ("hid", hid_hbm, hid), ("q", q_hbm, q), ("do", do_hbm, do), ("fo", fo_hbm, fo)
    )):
        loads[name] = pltpu.make_async_copy(src, dst, in_s.at[i])
        loads[name].start()
    loads["k"].wait()
    loads["v"].wait()
    pl.semaphore_wait(barrier, 6)

    def halo(name, slot, gi, srcs, to):
        cols = pl.ds(gi * 256, 256)
        for j in range(2):
            send(
                (name, gi, j), srcs[j].at[:, cols], kvr.at[slot, j, :, cols],
                kv_s.at[slot, gi, j], kv_r.at[slot, gi, j], to,
            )

    def one(gi):
        halo("one", 0, gi, (k, v), up)

    def pri(gi):
        halo("pri", 2, gi, (k, v), nxt)

    def fwd(gi):
        for j in range(2):
            cps["one", gi, j].wait_recv()
        halo("two", 1, gi, (kvr.at[0, 0], kvr.at[0, 1]), up)

    def turn():
        loads["hid"].wait()
        turned = hid[...].T
        for i in range(2 * RING):
            xt[i // 2, i % 2] = turned[i * ROWS : (i + 1) * ROWS]
        send("xc", xt.at[:, xh], xt_core, xt_s.at[0], xt_r.at[0], core)
        send("xf", xt.at[:, 1 - xh], xt_far.at[0], xt_s.at[1], xt_r.at[1], far)

    def xon():
        cps["xf"].wait_recv()
        send("xd", xt_far.at[0], xt_far.at[1], xt_s.at[2], xt_r.at[2], core)

    def xready():
        cps["xc"].wait_recv()
        cps["xd"].wait_recv()

    rows_i = lax.broadcasted_iota(jnp.int32, (TOK, TOK), 0)
    cols_i = lax.broadcasted_iota(jnp.int32, (TOK, TOK), 1)

    def block(outer_pos, inner_pos):
        return order[(outer_pos % n_outer) * RING + inner_pos % RING] * TOK

    def prep():
        starts = [jnp.int32(0)]
        for i in range(3):
            starts.append(starts[-1] + lengths[0, i])

        def doc_of(pos):
            total = jnp.zeros(pos.shape, jnp.int32)
            for s in starts:
                total = total + (pos >= s).astype(jnp.int32)
            return total

        qpos = block(oo, z) + cols_i
        qdoc = doc_of(qpos)
        slots = ((oo, z), (oo, z + RING - 1), (oo, z + RING - 2), (oo + n_outer - 1, z))
        for i, (a, b) in enumerate(slots):
            kpos = block(a, b) + rows_i
            live = (kpos <= qpos) & (doc_of(kpos) == qdoc)
            bias[i] = jnp.where(live, F32(0.0), F32(DEAD))
        angle = (block(oo, z) + rows_i).astype(F32) * inv[0:1, :]
        cosf[...] = jnp.cos(angle)
        sine = jnp.sin(angle)
        sinf[...] = jnp.where(cols_i < HD // 2, sine, -sine)
        for name in ("q", "do", "fo"):
            loads[name].wait()
        ones = jnp.ones((8, HD), BF16)
        for h in range(HQ):
            cols = slice(h * HD, (h + 1) * HD)
            prod = do[:, cols].astype(F32) * fo[:, cols].astype(F32)
            hi = prod.astype(BF16)
            lo = (prod - hi.astype(F32)).astype(BF16)
            delta[h : h + 1] = (nt(ones, hi) + nt(ones, lo))[0:1]

    def unrotate(grad):
        return grad * cosf[...] + pltpu.roll(grad, HD // 2, 1) * sinf[...]

    def attend(h, kk, vv, bb):
        a, b = slice(2 * h * HD, (2 * h + 1) * HD), slice((2 * h + 1) * HD, (2 * h + 2) * HD)
        qs = jnp.concatenate([q[:, a], q[:, b]], axis=0)
        dos = jnp.concatenate([do[:, a], do[:, b]], axis=0)
        lse_h = jnp.concatenate([lse[2 * h : 2 * h + 1], lse[2 * h + 1 : 2 * h + 2]], axis=1)
        delta_h = jnp.concatenate([delta[2 * h : 2 * h + 1], delta[2 * h + 1 : 2 * h + 2]], axis=1)
        capped = jnp.tanh(nt(kk, qs) * F32(1.0 / 600.0))
        prob = jnp.exp(F32(50.0) * capped - lse_h + jnp.concatenate([bb, bb], axis=1))
        dprob = nt(vv, dos)
        ds = (prob * (dprob - delta_h) * (F32(1.0 / 12.0) - F32(1.0 / 12.0) * (capped * capped))).astype(BF16)
        return tn(ds, kk), nn(ds, qs), nn(prob.astype(BF16), dos)

    def first(gi):
        for hh in range(2):
            h = gi * 2 + hh
            cols = slice(h * HD, (h + 1) * HD)
            kk = jnp.concatenate([k[:, cols], kvr[0, 0, :, cols]], axis=0)
            vv = jnp.concatenate([v[:, cols], kvr[0, 1, :, cols]], axis=0)
            dq, dk, dv = attend(h, kk, vv, bias[0:2].reshape(2 * TOK, TOK))
            dq_acc[h] = dq
            for j, val in enumerate((dk, dv)):
                home[gi, hh, j] = val[0:TOK]
                one_part[gi, hh, j] = val[TOK : 2 * TOK]

    def second(gi):
        for j in range(2):
            cps["two", gi, j].wait_recv()
            cps["pri", gi, j].wait_recv()
        for hh in range(2):
            h = gi * 2 + hh
            cols = slice(h * HD, (h + 1) * HD)
            kk = kvr[1:3, 0, :, cols].reshape(2 * TOK, HD)
            vv = kvr[1:3, 1, :, cols].reshape(2 * TOK, HD)
            dq, dk, dv = attend(h, kk, vv, bias[2:4].reshape(2 * TOK, TOK))
            for j, val in enumerate((dk, dv)):
                two_send[gi, hh, j] = val[0:TOK].astype(BF16)
                pri_send[gi, hh, j] = val[TOK : 2 * TOK].astype(BF16)
            total = dq_acc[h] + dq
            for i in range(2):
                at = (2 * h + i) * HD
                g[:, at : at + HD] = unrotate(total[i * TOK : (i + 1) * TOK]).astype(BF16)
        send(("ret", gi), two_send.at[gi], two_recv.at[gi], ret_s.at[1, gi], ret_r.at[1, gi], down)
        send(("rpri", gi), pri_send.at[gi], pri_recv.at[gi], ret_s.at[0, gi], ret_r.at[0, gi], prv)

    def carry(gi):
        cps["ret", gi].wait_recv()
        car_send[gi] = (two_recv[gi].astype(F32) + one_part[gi]).astype(BF16)
        send(("car", gi), car_send.at[gi], car_recv.at[gi], ret_s.at[2, gi], ret_r.at[2, gi], down)

    def settle(gi):
        cps["car", gi].wait_recv()
        cps["rpri", gi].wait_recv()
        for hh in range(2):
            h = gi * 2 + hh
            dk, dv = [
                home[gi, hh, j] + car_recv[gi, hh, j].astype(F32) + pri_recv[gi, hh, j].astype(F32)
                for j in range(2)
            ]
            at = HQ * HD + h * HD
            g[:, at : at + HD] = unrotate(dk).astype(BF16)
            at = (HQ + HK) * HD + h * HD
            g[:, at : at + HD] = dv.astype(BF16)

    def base(ch, who):
        lo, hi = CHUNKS[ch]
        return pl.ds(pl.multiple_of(lo + who * (hi - lo), HALF), HALF)

    def swap(ch):
        gq[ch, 0] = g[:, base(ch, c)]
        send(("g1", ch), g.at[:, base(ch, 1 - c)], gq.at[ch, 1], gx_s.at[ch, 0], gx_r.at[ch, 0], core)
        send(("g2", ch), gq.at[ch, 0], gq.at[ch, 2], gx_s.at[ch, 1], gx_r.at[ch, 1], far)

    def relay(ch):
        cps["g1", ch].wait_recv()
        send(("g3", ch), gq.at[ch, 1], gq.at[ch, 3], gx_s.at[ch, 2], gx_r.at[ch, 2], far)

    def term(ch, chain, s):
        way, hops = CHAINS[ch][chain]
        return part[ch, (z + 2 * RING + way * (hops - s)) % RING]

    def hop(ch, chain, s, val):
        rs_send[ch, chain, s] = val.astype(BF16)
        send(
            ("rs", ch, chain, s), rs_send.at[ch, chain, s], rs_recv.at[ch, chain, s],
            rs_ss.at[ch, chain, s], rs_rs.at[ch, chain, s], up if CHAINS[ch][chain][0] > 0 else down,
        )

    def mult(ch):
        cps["g2", ch].wait_recv()
        cps["g3", ch].wait_recv()
        gs = gq[ch].reshape(QUAD * TOK, HALF)
        for piece in range(2):
            at = slice(piece * 4, piece * 4 + 4)
            xs = jnp.concatenate(
                [xt.at[:, xh][at], xt_core[at], xt_far[0, at], xt_far[1, at]], axis=-1
            ).reshape(4 * ROWS, QUAD * TOK)
            part[ch, at] = nn(xs, gs).reshape(4, ROWS, HALF)
        for chain in range(2):
            hop(ch, chain, 0, term(ch, chain, 0))

    def step(ch, s):
        for chain in range(2):
            if s < CHAINS[ch][chain][1]:
                cps["rs", ch, chain, s - 1].wait_recv()
                hop(ch, chain, s, rs_recv[ch, chain, s - 1].astype(F32) + term(ch, chain, s))

    def finish(ch):
        val = part[ch, z]
        for chain in range(2):
            end = CHAINS[ch][chain][1] - 1
            cps["rs", ch, chain, end].wait_recv()
            val = val + rs_recv[ch, chain, end].astype(F32)
        fin[ch, 0] = val[0 : ROWS // 2]
        fin[ch, 1] = val[ROWS // 2 :]
        fin_send[ch] = fin[ch, 1 - c].astype(BF16)
        send(("fin", ch), fin_send.at[ch], fin_recv.at[ch], fin_s.at[ch], fin_r.at[ch], core)
        wout[:, base(ch, c)] = fin[ch, c].astype(BF16)

    def last(ch):
        cps["fin", ch].wait_recv()
        wout[:, base(ch, 1 - c)] = fin_recv[ch]

    steps = {
        "one": one, "pri": pri, "fwd": fwd, "turn": turn, "prep": prep, "xon": xon, "xready": xready,
        "first": first, "second": second, "carry": carry, "settle": settle, "swap": swap, "relay": relay,
        "mult": mult, "step": step, "finish": finish, "last": last,
    }
    settled = 0
    for name, *which in ORDER:
        steps[name](*which)
        if name in ("second", "settle"):
            settled += 1
            if settled == 2 * GROUPS:
                store = pltpu.make_async_copy(g, gout, in_s.at[6])
                store.start()
    store.wait()
    for cp in sends:
        cp.wait_send()


def local(hidden_in, queries, keys, values, fwd_out, out_grad, lse, block_order, doc_lengths):
    freq = 10000.0 ** (-2.0 * np.arange(HD // 2, dtype=np.float32) / HD)
    inv = jnp.asarray(np.broadcast_to(np.concatenate([freq, freq])[None, :], (8, HD)).astype(np.float32))
    vm = pl.BlockSpec(memory_space=pltpu.VMEM)
    sm = pl.BlockSpec(memory_space=pltpu.SMEM)
    hbm = pl.BlockSpec(memory_space=pl.ANY)
    ret = pltpu.VMEM((GROUPS, 2, 2, TOK, HD), BF16)
    dma = pltpu.SemaphoreType.DMA
    nch = len(CHUNKS)
    qkv, weights = pl.pallas_call(
        kernel,
        out_shape=(
            jax.ShapeDtypeStruct((TOK, COLS), BF16),
            jax.ShapeDtypeStruct((ROWS // 2, COLS), BF16),
        ),
        in_specs=[hbm] * 6 + [vm, sm, sm, vm],
        out_specs=(hbm, vm),
        scratch_shapes=[
            pltpu.VMEM((TOK, D), BF16),
            pltpu.VMEM((TOK, HQ * HD), BF16),
            pltpu.VMEM((TOK, HK * HD), BF16),
            pltpu.VMEM((TOK, HK * HD), BF16),
            pltpu.VMEM((TOK, HQ * HD), BF16),
            pltpu.VMEM((TOK, HQ * HD), BF16),
            pltpu.VMEM((3, 2, TOK, HK * HD), BF16),
            pltpu.VMEM((4, TOK, TOK), F32),
            pltpu.VMEM((TOK, HD), F32),
            pltpu.VMEM((TOK, HD), F32),
            pltpu.VMEM((HQ, TOK), F32),
            pltpu.VMEM((HK, 2 * TOK, HD), F32),
            pltpu.VMEM((GROUPS, 2, 2, TOK, HD), F32),
            pltpu.VMEM((GROUPS, 2, 2, TOK, HD), F32),
            ret, ret, ret, ret, ret, ret,
            pltpu.VMEM((TOK, COLS), BF16),
            pltpu.VMEM((RING, 2, ROWS, TOK), BF16),
            pltpu.VMEM((RING, ROWS, TOK), BF16),
            pltpu.VMEM((2, RING, ROWS, TOK), BF16),
            pltpu.VMEM((nch, QUAD, TOK, HALF), BF16),
            pltpu.VMEM((nch, RING, ROWS, HALF), F32),
            pltpu.VMEM((nch, 2, 4, ROWS, HALF), BF16),
            pltpu.VMEM((nch, 2, 4, ROWS, HALF), BF16),
            pltpu.VMEM((nch, 2, ROWS // 2, HALF), F32),
            pltpu.VMEM((nch, ROWS // 2, HALF), BF16),
            pltpu.VMEM((nch, ROWS // 2, HALF), BF16),
            dma((7,)),
            dma((3, GROUPS, 2)), dma((3, GROUPS, 2)),
            dma((3, GROUPS)), dma((3, GROUPS)),
            dma((3,)), dma((3,)),
            dma((nch, 3)), dma((nch, 3)),
            dma((nch, 2, 4)), dma((nch, 2, 4)),
            dma((nch,)), dma((nch,)),
        ],
        compiler_params=pltpu.CompilerParams(
            collective_id=0, has_side_effects=True, vmem_limit_bytes=58 * 1024 * 1024
        ),
        cost_estimate=pl.CostEstimate(flops=4 * 10**9, bytes_accessed=6 * 10**6, transcendentals=2 * 10**6),
    )(
        hidden_in[0], queries[0], keys[0], values[0], fwd_out[0], out_grad[0], lse[0],
        block_order, doc_lengths, inv,
    )
    return (qkv[None], weights[None])


def solution(mesh):
    tokens = P("fsdp", ("outer", "inner"), None)
    in_specs = (tokens,) * 6 + (P("fsdp", None, ("outer", "inner")), P(), P("fsdp", None))
    out_specs = (tokens, P("outer", ("inner", "fsdp"), None))
    return jax.shard_map(local, mesh=mesh, in_specs=in_specs, out_specs=out_specs, check_vma=False)
```

time: 115 us -> 99.6 us (0.87)
  Pallas kernels: 111 us -> 95.6 us
    pallas_call x1, Pallas kernels: 111 us -> 95.6 us  [local(): pl.pallas_call(kernel, out_shape=(jax.ShapeDtypeStruct((TOK, COLS), BF16)...]
where the time goes in v2:
time: 99.6 us; the launch traced here: 99.4 us
  Pallas kernels  95.6 us (96%)
  local copies, waits for them, and re-layouts  3.17 us (3%)
    pallas_call x1, Pallas kernels, local(): pl.pallas_call(kernel, out_shape=(jax.ShapeDtypeStruct((TOK, COLS), BF16)...  95.6 us
    unnamed x4, local copies, waits for them, and re-layouts  3.17 us

profile of v2, /device:TPU:1, one launch (start us, length us, event | category | flops | bytes accessed | tf_op | source)
XLA Modules:
  0.0 99.4 jit_solution(8298096795683275774)
XLA Ops:
  0.6 95.6 %shard_map.113 = (bf16[128,4096]{1,0:T(8,128)(2,1)}, bf16[72,4096]{1,0:T(8,128)(2,1)}) custom-call(bf16[128,2304]{1,0:T(8,128)(2,1)} %bitcast.11, bf16[128,2048]{1,0:T(8,128)(2,1)} %bitcast.12, bf16[128,1024]{1,0:T(8,128)(2,1)} %bitcast.15, bf16[128,1024]{1,0:T(8,128)(2,1)} %bitcast.16, bf16[128,2048]{1,0:T(8,128)(2,1)} %bitcast.13, ...), custom_call_target="tpu_custom_call" | custom-call | flops 4000000000 | bytes 6000000 | tf_op jit(solution)/shard_map/pallas_call | solution.py:334
  96.3 0.0 copy-start
  96.3 2.3 %copy.14 = bf16[1,128,4096]{2,1,0:T(8,128)(2,1)} copy(bf16[1,128,4096]{2,1,0:T(8,128)(2,1)} %bitcast.9) | data formatting | bytes 2097152
  98.6 0.0 copy-done
  98.6 0.8 copy.15
Async XLA Ops:
  96.3 2.4 %copy-start = (bf16[72,4096]{1,0:T(8,128)(2,1)S(1)}, bf16[72,4096]{1,0:T(8,128)(2,1)}, u32[]{:S(2)}) copy-start(bf16[72,4096]{1,0:T(8,128)(2,1)} %get-tuple-element.5) | copy-start | bytes 1769476

commit v3 on v2

--- a/solution.py
+++ b/solution.py
@@ -30,7 +30,7 @@
 )
 LONG_UP = ((1, 4), (-1, 3))
 LONG_DOWN = ((1, 3), (-1, 4))
-CHAINS = (LONG_UP, LONG_DOWN, LONG_UP, LONG_UP, LONG_DOWN, LONG_UP, LONG_UP, LONG_UP)
+CHAINS = (LONG_UP, LONG_UP, LONG_UP, LONG_DOWN, LONG_UP, LONG_DOWN, LONG_UP, LONG_DOWN)
 ORDER = (
     ("pri", 0), ("pri", 2), ("one", 2), ("turn",), ("prep",), ("one", 0), ("fwd", 2), ("first", 2), ("fwd", 0),
     ("first", 0), ("second", 2), ("swap", 2), ("relay", 2), ("one", 1), ("pri", 1), ("second", 0), ("swap", 0),
@@ -61,9 +61,9 @@
 
 
 def kernel(
-    hid_hbm, q_hbm, k_hbm, v_hbm, fo_hbm, do_hbm, lse, order, lengths, inv,
+    hid_hbm, q_hbm, k_hbm, v_hbm, fo_hbm, do_hbm, lse_hbm, order_hbm, lengths_hbm, inv_hbm,
     gout, wout,
-    hid, q, k, v, fo, do,
+    hid, q, k, v, fo, do, lse, inv, order, lengths,
     kvr, bias, cosf, sinf, delta, dq_acc, home, one_part,
     two_send, two_recv, car_send, car_recv, pri_send, pri_recv,
     g, xt, xt_core, xt_far, gq, part, rs_send, rs_recv, fin, fin_send, fin_recv,
@@ -98,7 +98,9 @@
         pl.semaphore_signal(barrier, inc=1, device_id=to, device_id_type=MESH)
     loads = {}
     for i, (name, src, dst) in enumerate((
-        ("k", k_hbm, k), ("v", v_hbm, v), ("hid", hid_hbm, hid), ("q", q_hbm, q), ("do", do_hbm, do), ("fo", fo_hbm, fo)
+        ("k", k_hbm, k), ("v", v_hbm, v), ("hid", hid_hbm, hid), ("q", q_hbm, q), ("do", do_hbm, do), ("fo", fo_hbm, fo),
+        ("lse", lse_hbm, lse), ("inv", inv_hbm, inv),
+        ("order", order_hbm, order), ("lengths", lengths_hbm, lengths),
     )):
         loads[name] = pltpu.make_async_copy(src, dst, in_s.at[i])
         loads[name].start()
@@ -148,6 +150,8 @@
         return order[(outer_pos % n_outer) * RING + inner_pos % RING] * TOK
 
     def prep():
+        loads["order"].wait()
+        loads["lengths"].wait()
         starts = [jnp.int32(0)]
         for i in range(3):
             starts.append(starts[-1] + lengths[0, i])
@@ -165,6 +169,8 @@
             kpos = block(a, b) + rows_i
             live = (kpos <= qpos) & (doc_of(kpos) == qdoc)
             bias[i] = jnp.where(live, F32(0.0), F32(DEAD))
+        loads["inv"].wait()
+        loads["lse"].wait()
         angle = (block(oo, z) + rows_i).astype(F32) * inv[0:1, :]
         cosf[...] = jnp.cos(angle)
         sine = jnp.sin(angle)
@@ -315,11 +321,16 @@
         if name in ("second", "settle"):
             settled += 1
             if settled == 2 * GROUPS:
-                store = pltpu.make_async_copy(g, gout, in_s.at[6])
+                store = pltpu.make_async_copy(g, gout, in_s.at[10])
                 store.start()
     store.wait()
     for cp in sends:
         cp.wait_send()
+
+
+def hand_over(qkv, weights, qkv_out, weights_out):
+    qkv_out[...] = qkv[...]
+    weights_out[...] = weights[...]
 
 
 def local(hidden_in, queries, keys, values, fwd_out, out_grad, lse, block_order, doc_lengths):
@@ -337,7 +348,7 @@
             jax.ShapeDtypeStruct((TOK, COLS), BF16),
             jax.ShapeDtypeStruct((ROWS // 2, COLS), BF16),
         ),
-        in_specs=[hbm] * 6 + [vm, sm, sm, vm],
+        in_specs=[hbm] * 10,
         out_specs=(hbm, vm),
         scratch_shapes=[
             pltpu.VMEM((TOK, D), BF16),
@@ -346,6 +357,10 @@
             pltpu.VMEM((TOK, HK * HD), BF16),
             pltpu.VMEM((TOK, HQ * HD), BF16),
             pltpu.VMEM((TOK, HQ * HD), BF16),
+            pltpu.VMEM((HQ, TOK), F32),
+            pltpu.VMEM((8, HD), F32),
+            pltpu.SMEM((64,), jnp.int32),
+            pltpu.SMEM((1, 4), jnp.int32),
             pltpu.VMEM((3, 2, TOK, HK * HD), BF16),
             pltpu.VMEM((4, TOK, TOK), F32),
             pltpu.VMEM((TOK, HD), F32),
@@ -366,7 +381,7 @@
             pltpu.VMEM((nch, 2, ROWS // 2, HALF), F32),
             pltpu.VMEM((nch, ROWS // 2, HALF), BF16),
             pltpu.VMEM((nch, ROWS // 2, HALF), BF16),
-            dma((7,)),
+            dma((11,)),
             dma((3, GROUPS, 2)), dma((3, GROUPS, 2)),
             dma((3, GROUPS)), dma((3, GROUPS)),
             dma((3,)), dma((3,)),
@@ -382,6 +397,18 @@
         hidden_in[0], queries[0], keys[0], values[0], fwd_out[0], out_grad[0], lse[0],
         block_order, doc_lengths, inv,
     )
+    pieces = 2
+    blocks = [pl.BlockSpec((TOK, COLS // pieces), lambda i: (0, i)), pl.BlockSpec((ROWS // 2, COLS // pieces), lambda i: (0, i))]
+    qkv, weights = pl.pallas_call(
+        hand_over,
+        out_shape=(
+            jax.ShapeDtypeStruct((TOK, COLS), BF16),
+            jax.ShapeDtypeStruct((ROWS // 2, COLS), BF16),
+        ),
+        grid=(pieces,),
+        in_specs=blocks,
+        out_specs=blocks,
+    )(qkv, weights)
     return (qkv[None], weights[None])
 
 

time: 99.6 us -> 96.5 us (0.969)
  local copies, waits for them, and re-layouts: 3.17 us -> 0 us
    unnamed x4 -> x0, local copies, waits for them, and re-layouts: 3.17 us -> none
    pallas_call x0 -> x1, Pallas kernels: none -> 2.34 us  [local(): pl.pallas_call(hand_over, out_shape=(jax.ShapeDtypeStruct((TOK, COLS), BF...]
    pallas_call x1, Pallas kernels: 95.6 us -> 93.4 us  [local(): pl.pallas_call(kernel, out_shape=(jax.ShapeDtypeStruct((TOK, COLS), BF16)...]
where the time goes in v3:
time: 96.5 us; the launch traced here: 96.4 us
  Pallas kernels  95.8 us (99%)
    pallas_call x1, Pallas kernels, local(): pl.pallas_call(kernel, out_shape=(jax.ShapeDtypeStruct((TOK, COLS), BF16)...  93.4 us
    pallas_call x1, Pallas kernels, local(): pl.pallas_call(hand_over, out_shape=(jax.ShapeDtypeStruct((TOK, COLS), BF...  2.34 us

profile of v3, /device:TPU:1, one launch (start us, length us, event | category | flops | bytes accessed | tf_op | source)
XLA Modules:
  0.0 96.4 jit_solution(10486389801963393307)
XLA Ops:
  0.6 93.4 %shard_map.113 = (bf16[128,4096]{1,0:T(8,128)(2,1)}, bf16[72,4096]{1,0:T(8,128)(2,1)}) custom-call(bf16[128,2304]{1,0:T(8,128)(2,1)} %bitcast.10, bf16[128,2048]{1,0:T(8,128)(2,1)} %bitcast.12, bf16[128,1024]{1,0:T(8,128)(2,1)} %bitcast.15, bf16[128,1024]{1,0:T(8,128)(2,1)} %bitcast.16, bf16[128,2048]{1,0:T(8,128)(2,1)} %bitcast.13, ...), custom_call_target="tpu_custom_call" | custom-call | flops 4000000000 | bytes 6000000 | tf_op jit(solution)/shard_map/pallas_call | solution.py:345
  94.1 2.3 %shard_map.114 = (bf16[128,4096]{1,0:T(8,128)(2,1)}, bf16[72,4096]{1,0:T(8,128)(2,1)}) custom-call(bf16[128,4096]{1,0:T(8,128)(2,1)} %get-tuple-element.6.qkv, bf16[72,4096]{1,0:T(8,128)(2,1)} %get-tuple-element.7.weights), custom_call_target="tpu_custom_call" | custom-call | tf_op jit(solution)/shard_map/pallas_call | solution.py:402

commit v4 on v3

--- a/solution.py
+++ b/solution.py
@@ -230,7 +230,6 @@
                 at = (2 * h + i) * HD
                 g[:, at : at + HD] = unrotate(total[i * TOK : (i + 1) * TOK]).astype(BF16)
         send(("ret", gi), two_send.at[gi], two_recv.at[gi], ret_s.at[1, gi], ret_r.at[1, gi], down)
-        send(("rpri", gi), pri_send.at[gi], pri_recv.at[gi], ret_s.at[0, gi], ret_r.at[0, gi], prv)
 
     def carry(gi):
         cps["ret", gi].wait_recv()
@@ -259,6 +258,10 @@
         gq[ch, 0] = g[:, base(ch, c)]
         send(("g1", ch), g.at[:, base(ch, 1 - c)], gq.at[ch, 1], gx_s.at[ch, 0], gx_r.at[ch, 0], core)
         send(("g2", ch), gq.at[ch, 0], gq.at[ch, 2], gx_s.at[ch, 1], gx_r.at[ch, 1], far)
+        if ch < GROUPS:
+            send(
+                ("rpri", ch), pri_send.at[ch], pri_recv.at[ch], ret_s.at[0, ch], ret_r.at[0, ch], prv
+            )
 
     def relay(ch):
         cps["g1", ch].wait_recv()

time: 96.5 us -> 96.5 us (level)
  no operation moved by 1% of the time
where the time goes in v4:
time: 96.5 us; the launch traced here: 96.4 us
  Pallas kernels  95.7 us (99%)
    pallas_call x1, Pallas kernels, local(): pl.pallas_call(kernel, out_shape=(jax.ShapeDtypeStruct((TOK, COLS), BF16)...  93.4 us
    pallas_call x1, Pallas kernels, local(): pl.pallas_call(hand_over, out_shape=(jax.ShapeDtypeStruct((TOK, COLS), BF...  2.34 us

profile of v4, /device:TPU:1, one launch (start us, length us, event | category | flops | bytes accessed | tf_op | source)
XLA Modules:
  0.0 96.4 jit_solution(7540872011530746175)
XLA Ops:
  0.6 93.4 %shard_map.113 = (bf16[128,4096]{1,0:T(8,128)(2,1)}, bf16[72,4096]{1,0:T(8,128)(2,1)}) custom-call(bf16[128,2304]{1,0:T(8,128)(2,1)} %bitcast.10, bf16[128,2048]{1,0:T(8,128)(2,1)} %bitcast.12, bf16[128,1024]{1,0:T(8,128)(2,1)} %bitcast.15, bf16[128,1024]{1,0:T(8,128)(2,1)} %bitcast.16, bf16[128,2048]{1,0:T(8,128)(2,1)} %bitcast.13, ...), custom_call_target="tpu_custom_call" | custom-call | flops 4000000000 | bytes 6000000 | tf_op jit(solution)/shard_map/pallas_call | solution.py:348
  94.0 2.3 %shard_map.114 = (bf16[128,4096]{1,0:T(8,128)(2,1)}, bf16[72,4096]{1,0:T(8,128)(2,1)}) custom-call(bf16[128,4096]{1,0:T(8,128)(2,1)} %get-tuple-element.6.qkv, bf16[72,4096]{1,0:T(8,128)(2,1)} %get-tuple-element.7.weights), custom_call_target="tpu_custom_call" | custom-call | tf_op jit(solution)/shard_map/pallas_call | solution.py:405
